TPU v7x, 256 devices: a whole 4x4x8 slice. The times are simulated.
256 devices in a mesh: group: 8 (over z_lo, x), tp: 32 (over z_hi, y, core).
Axes of the slice: x: 4, y: 4, z: 8 (z_hi: 4, z_lo: 2; z = z_hi * 2 + z_lo), core: 2. Of those that a mesh axis runs over, the one named last changes fastest.
Arguments:
- tokens: bfloat16 [3584, 6144], P('group'), may hold values from -6 to 6
- routes: int32 [3584, 2], P('group'), may hold values from 0 to 7, as said below
- route_weights: float32 [3584, 2], P('group'), may hold values from 0.25 to 1
- ffn_weights: bfloat16 [1, 3, 6144, 8, 2048], P(None, None, 'tp', 'group'), may hold values from -0.078125 to 0.078125
Outputs:
- mixed: bfloat16 [3584, 6144], P(('group', 'tp'))
Inputs may be any that keep to these rules, and one draw needn't show every extreme that they name: `routes`: each row names two different experts. Expert 0 is named by at most 392 of one group's 448 rows.
All inputs are finite; a program needn't handle non-finite values.
Results may differ from a plain program's by a relative error of at most 0.024.
Values may be sent and summed in bfloat16 or wider, within the bound.
A program may use at most 128 MiB of HBM per device.

v0:
```python
import jax
import jax.numpy as jnp
from jax import lax
from jax.sharding import PartitionSpec as P


def per_device(tokens, routes, route_weights, ffn_weights):
    row_count = tokens.shape[0]
    feature_count = tokens.shape[1]
    matched = routes == 0
    member = jnp.any(matched, axis=1)
    mix_column = jnp.sum(jnp.where(matched, route_weights, 0.0), axis=1)
    tile_rows = row_count * 7 // 8
    iota_tokens = jnp.arange(row_count, dtype=jnp.int32)
    iota_slots = jnp.arange(tile_rows, dtype=jnp.int32)
    slot_ids = jnp.cumsum(member.astype(jnp.int32)) - 1
    selector = (slot_ids[None, :] == iota_slots[:, None]) & member[None, :]
    row_index = jnp.sum(jnp.where(selector, iota_tokens[None, :], 0), axis=1)
    tiles = tokens[row_index]
    slot_index = jnp.maximum(slot_ids, 0)
    row_sliced = lax.all_to_all(ffn_weights, "tp", split_axis=4, concat_axis=2, tiled=True)
    row_sliced = row_sliced[0]
    full_slice = lax.all_gather(row_sliced, "group", axis=2, tiled=True)
    shard_piece = full_slice[None]
    unit_count = shard_piece.shape[3] * shard_piece.shape[4]
    flat = shard_piece.reshape(3, feature_count, unit_count)
    gate_out = jnp.dot(tiles, flat[0], preferred_element_type=jnp.float32)
    up_out = jnp.dot(tiles, flat[1], preferred_element_type=jnp.float32)
    hidden = (jax.nn.silu(gate_out) * up_out).astype(jnp.bfloat16)
    expert_out = lax.dot_general(
        hidden, flat[2], (((1,), (1,)), ((), ())), preferred_element_type=jnp.float32
    )
    placed = expert_out[slot_index]
    summed = mix_column[:, None] * placed
    reduced = lax.psum_scatter(summed.astype(jnp.bfloat16), "tp", scatter_dimension=0, tiled=True)
    return reduced


def solution(mesh):
    placed = (
        P("group", None),
        P("group", None),
        P("group", None),
        P(None, None, "tp", "group", None),
    )
    return jax.shard_map(
        per_device, mesh=mesh, in_specs=placed, out_specs=P(("group", "tp"), None), check_vma=False
    )
```

profile of v0, /device:TPU:169, one launch (start us, length us, event | category | flops | bytes accessed | tf_op | source)
XLA Modules:
  0.0 493.3 jit_solution(14475798323674064570)
XLA Ops:
  6.5 0.0 all-gather.2.cloned.1.call-start
  6.5 6.9 %copy.13 = bf16[1,3,192,1,2048]{2,1,3,0,4:T(4,128)(2,1)} copy(bf16[1,3,192,1,2048]{4,2,3,1,0:T(8,128)(2,1)} %param.7) | data formatting | bytes 4718592 | tf_op args[3]
  13.5 101.8 %all_to_all.15 = bf16[1,3,192,1,2048]{2,1,3,0,4:T(4,128)(2,1)S(1)} all-to-all(bf16[1,3,192,1,2048]{2,1,3,0,4:T(4,128)(2,1)} %copy.13), channel_id=1, replica_groups=mesh['group'=8,'tp'=32] {'tp'}, dimensions={4} | all-to-all | bytes 4718592 | tf_op jit(solution)/shard_map/all_to_all | solution.py:21
  115.2 0.4 copy.14
  115.7 0.0 copy-start.1
  115.7 1.8 copy.15
  117.5 4.3 squeeze.12
  121.8 0.0 all-gather.2.cloned.1.call-update
  121.8 0.0 copy-done.1
  121.9 0.3 reduce-window.9
  122.2 0.1 slice.22
  122.3 0.1 slice_reduce_fusion
  122.4 0.1 add_bitcast_fusion
  122.5 0.3 select_reduce_fusion
  122.8 0.0 copy-start.2
  122.8 15.0 %gather_fusion = bf16[392,6144]{1,0:T(8,128)(2,1)} fusion(bf16[448,6144]{1,0:T(8,128)(2,1)} %param.4, s32[1024]{0:T(1024)S(1)} %pad_clamp_fusion.1), kind=kCustom, calls=%fused_computation | custom fusion | bytes 9635360 | tf_op jit(solution)/shard_map/gather | solution.py:19
  137.8 0.0 copy-done.2
  137.8 177.6 %all-gather.2.cloned.1.call-done = bf16[3,6144,8,64]{1,3,0,2:T(8,128)(2,1)} async-done(((bf16[3,6144,1,64]{1,3,0,2:T(8,128)(2,1)}), bf16[3,6144,8,64]{1,3,0,2:T(8,128)(2,1)}) %all-gather.2.cloned.1.call-update) | async-done | bytes 18874384 | tf_op jit(solution)/shard_map/all_gather | solution.py:23
  315.4 0.0 copy-start
  315.4 8.5 %fusion.4 = (bf16[1,6144,8,64]{1,3,0,2:T(8,128)(2,1)S(1)}, bf16[1,6144,8,64]{1,3,0,2:T(8,128)(2,1)S(1)}, bf16[1,6144,8,64]{1,3,0,2:T(8,128)(2,1)S(1)}) fusion(bf16[3,6144,8,64]{1,3,0,2:T(8,128)(2,1)} %all-gather.2.cloned.1.call-done), kind=kLoop, calls=%fused_computation.20 | loop fusion | bytes 37748736 | tf_op jit(solution)/shard_map/slice | solution.py:31
  323.9 0.0 copy-done
  323.9 2.7 fusion.5
  326.6 2.7 fusion.1
  329.3 5.1 %fusion.6 = f32[392,6144]{1,0:T(8,128)} fusion(bf16[392,512]{1,0:T(8,128)(2,1)S(1)} %fusion.1, bf16[6144,512]{0,1:T(8,128)(2,1)S(1)} %bitcast.31), kind=kOutput, calls=%fused_computation.22 | convolution fusion | flops 2466250752 | bytes 16326656 | tf_op jit(solution)/shard_map/dot_general | solution.py:30
  334.4 15.9 %gather_fusion.1 = f32[448,6144]{1,0:T(8,128)} fusion(f32[392,6144]{1,0:T(8,128)} %fusion.6, s32[1024]{0:T(1024)S(1)} %pad_clamp_fusion), kind=kCustom, calls=%fused_computation.1 | custom fusion | bytes 22021888 | tf_op jit(solution)/shard_map/gather | solution.py:33
  350.3 0.0 copy-start.3
  350.3 8.1 %multiply_convert_fusion = bf16[448,6144]{1,0:T(8,128)(2,1)} fusion(f32[448,6144]{1,0:T(8,128)} %gather_fusion.1, f32[448]{0:T(512)S(1)} %select_reduce_fusion.1), kind=kLoop, calls=%fused_computation.2 | loop fusion | flops 5505024 | bytes 16516864 | tf_op jit(solution)/shard_map/convert_element_type | solution.py:35
  358.3 81.4 %fusion = bf16[16,6144]{1,0:T(8,128)(2,1)S(1)} fusion(bf16[448,6144]{1,0:T(8,128)(2,1)} %multiply_convert_fusion), kind=kCustom, calls=%all-reduce-scatter | all-reduce-scatter fusion | flops 3145729 | bytes 5702656
  439.8 6.1 %collective-permute-start.2 = (bf16[16,6144]{1,0:T(8,128)(2,1)S(1)}, bf16[16,6144]{1,0:T(8,128)(2,1)S(1)}, u32[]{:S(2)}, u32[]{:S(2)}) collective-permute-start(bf16[16,6144]{1,0:T(8,128)(2,1)S(1)} %fusion), channel_id=1, source_target_pairs={{0,3},{1,4},{2,5},{3,6},{4,7},{5,8},{6,9},{7,10},{8,11},{9,12},{10... | collective-permute-start | bytes 589832
  445.9 11.3 %collective-permute-start.1 = (bf16[16,6144]{1,0:T(8,128)(2,1)S(1)}, bf16[16,6144]{1,0:T(8,128)(2,1)S(1)}, u32[]{:S(2)}, u32[]{:S(2)}) collective-permute-start(bf16[16,6144]{1,0:T(8,128)(2,1)S(1)} %fusion), channel_id=1, source_target_pairs={{0,2},{1,3},{2,4},{3,5},{4,6},{5,7},{6,8},{7,9},{8,10},{9,11},{10,... | collective-permute-start | bytes 589832
  457.2 1.9 collective-permute-start
  459.2 2.5 collective-permute-start.3
  461.7 0.0 copy-done.3
  461.7 0.6 dynamic-slice.4
  462.9 20.7 %collective-permute-done.3 = bf16[14,6144]{1,0:T(8,128)(2,1)S(1)} collective-permute-done((bf16[14,6144]{1,0:T(8,128)(2,1)S(1)}, bf16[14,6144]{1,0:T(8,128)(2,1)S(1)}, u32[]{:S(2)}, u32[]{:S(2)}) %collective-permute-start.3) | collective-permute-done | bytes 172064
  483.6 0.0 collective-permute-done.2
  483.6 0.0 collective-permute-done.1
  483.6 0.0 collective-permute-done
  483.6 2.1 concatenate
  485.7 0.7 constant_dynamic-slice_fusion
  (9 shorter events, 0.2 us)
Async XLA Ops:
  6.5 308.9 %all-gather.2.cloned.1.call-start = ((), (), s32[]{:S(2)}) async-start(), calls=%async_computation.1 | async-start | bytes 21233664 | tf_op jit(solution)/shard_map/all_gather | solution.py:23
  115.7 6.1 %copy-start.1 = (s32[448,2]{0,1:T(2,128)S(1)}, s32[448,2]{0,1:T(2,128)}, u32[]{:S(2)}) copy-start(s32[448,2]{0,1:T(2,128)} %param.5) | copy-start | bytes 10756
  122.8 15.1 %copy-start.2 = (f32[448,2]{0,1:T(2,128)S(1)}, f32[448,2]{0,1:T(2,128)}, u32[]{:S(2)}) copy-start(f32[448,2]{0,1:T(2,128)} %param.6) | copy-start | bytes 10756
  315.4 8.5 %copy-start = (bf16[392,6144]{1,0:T(8,128)(2,1)S(1)}, bf16[392,6144]{1,0:T(8,128)(2,1)}, u32[]{:S(2)}) copy-start(bf16[392,6144]{1,0:T(8,128)(2,1)} %gather_fusion) | copy-start | bytes 14450692
  350.3 111.4 %copy-start.3 = (u32[256]{0:T(256)S(1)}, u32[256]{0:T(256)}, u32[]{:S(2)}) copy-start(u32[256]{0:T(256)} %constant.28) | copy-start | bytes 3076
  439.8 43.8 %collective-permute-start.2 = (bf16[16,6144]{1,0:T(8,128)(2,1)S(1)}, bf16[16,6144]{1,0:T(8,128)(2,1)S(1)}, u32[]{:S(2)}, u32[]{:S(2)}) collective-permute-start(bf16[16,6144]{1,0:T(8,128)(2,1)S(1)} %fusion), channel_id=1, source_target_pairs={{0,3},{1,4},{2,5},{3,6},{4,7},{5,8},{6,9},{7,10},{8,11},{9,12},{10... | collective-permute-start | bytes 589832
  445.9 37.7 %collective-permute-start.1 = (bf16[16,6144]{1,0:T(8,128)(2,1)S(1)}, bf16[16,6144]{1,0:T(8,128)(2,1)S(1)}, u32[]{:S(2)}, u32[]{:S(2)}) collective-permute-start(bf16[16,6144]{1,0:T(8,128)(2,1)S(1)} %fusion), channel_id=1, source_target_pairs={{0,2},{1,3},{2,4},{3,5},{4,6},{5,7},{6,8},{7,9},{8,10},{9,11},{10,... | collective-permute-start | bytes 589832
  457.2 26.4 %collective-permute-start = (bf16[16,6144]{1,0:T(8,128)(2,1)S(1)}, bf16[16,6144]{1,0:T(8,128)(2,1)S(1)}, u32[]{:S(2)}, u32[]{:S(2)}) collective-permute-start(bf16[16,6144]{1,0:T(8,128)(2,1)S(1)} %fusion), channel_id=1, source_target_pairs={{0,1},{1,2},{2,3},{3,4},{4,5},{5,6},{6,7},{7,8},{8,9},{9,10},{10,1... | collective-permute-start | bytes 589832
  459.2 24.4 %collective-permute-start.3 = (bf16[14,6144]{1,0:T(8,128)(2,1)S(1)}, bf16[14,6144]{1,0:T(8,128)(2,1)S(1)}, u32[]{:S(2)}, u32[]{:S(2)}) collective-permute-start(bf16[14,6144]{1,0:T(8,128)(2,1)S(1)} %slice.35), channel_id=1, source_target_pairs={{0,4},{1,5},{2,6},{3,7},{4,8},{5,9},{6,10},{7,11},{8,12},{9,13},{1... | collective-permute-start | bytes 516104
Sparse Core Ops, SparseCore 0:
  121.9 193.4 all-gather.1
where the time goes:
time: 494 us; the launch traced here: 493 us
  waiting for transfers between devices  198 us (40%)
  blocking collectives  183 us (37%)
  local copies, waits for them, and re-layouts  56.5 us (11%)
  starting transfers between devices  21.8 us (4%)
  between operations  14.2 us (3%)
  matrix products  10.5 us (2%)
  other arithmetic  8.81 us (2%)
    all_gather x1, waiting for transfers between devices, per_device(): full_slice = lax.all_gather(row_sliced, 'group', axis=2, tiled=True)  178 us
    all_to_all x1, blocking collectives, per_device(): lax.all_to_all(ffn_weights, 'tp', split_axis=4, concat_axis=2, tiled=True)  102 us
    unnamed x1, blocking collectives  81.4 us
    unnamed x4, starting transfers between devices  21.8 us
    unnamed x5, waiting for transfers between devices  20.7 us
    gather x1, local copies, waits for them, and re-layouts, per_device(): placed = expert_out[slot_index]  15.9 us
    gather x1, local copies, waits for them, and re-layouts, per_device(): tiles = tokens[row_index]  15 us
    unnamed x13, local copies, waits for them, and re-layouts  10.5 us
  transfers between devices with their start and end apart: 5, of which 2 were waited for; matrix products, arithmetic and copies ran while one was open for 3% of the time, Pallas kernels for 0%

commit v1 on v0

v1 whole, which is shorter than its diff:
```python
import jax
import jax.numpy as jnp
from jax import lax
from jax.experimental import pallas as pl
from jax.experimental.pallas import tpu as pltpu
from jax.sharding import PartitionSpec as P

MESH = pl.DeviceIdType.MESH
NX, NY, NZ, NC = 4, 4, 8, 2
OWN = 14
PAD = 16


def dev(x, y, z, c):
    x, y, z = lax.rem(x + 2 * NX, NX), lax.rem(y + 2 * NY, NY), lax.rem(z + 2 * NZ, NZ)
    return ((z % 2) * NX + x, ((z // 2) * NY + y) * NC + c)


def take(ref, sem):
    pltpu.make_async_copy(ref, ref, sem).wait()


def kernel(tok_hbm, w_hbm, out_ref, tok, gu, wd, px, pr, po, hid, acc, st, rv, fin, fo,
           tok_sem, tk_ss, tk_rs, a_ss, a_rs, xo_ss, x_rs, xf_ss, w_ss, w_rs, wo_ss, wx_rs, wf_ss,
           p_ss, p_rs, h_ss, h_rs, s_ss, s_rs, r_ss, r_rs, f_ss, f_rs):
    grp, tp = lax.axis_index("group"), lax.axis_index("tp")
    z_lo, x = grp // NX, grp % NX
    c, y, z_hi = tp % NC, (tp // NC) % NY, tp // (NC * NY)
    z = z_hi * 2 + z_lo
    rows = tok.shape[1]
    half = tok.shape[2]
    piece = w_hbm.shape[1]
    hrows = rows // 2
    dcols = acc.shape[2]

    def send(src, dst, ss, rs, to):
        pltpu.make_async_remote_copy(
            src_ref=src, dst_ref=dst, send_sem=ss, recv_sem=rs, device_id=to, device_id_type=MESH
        ).start()

    right, left = dev(x + 1, y, z, c), dev(x - 1, y, z, c)
    up, down = dev(x, y, z + 1, c), dev(x, y, z - 1, c)
    sib = dev(x, y, z, 1 - c)
    mycols = pl.ds(pl.multiple_of(c * half, 128), half)
    load = pltpu.make_async_copy(tok_hbm.at[:, mycols], tok.at[z_lo], tok_sem)
    load.start()

    bar = pltpu.get_barrier_semaphore()
    me = (z * NY + y) * NC + c
    plane = NZ * NY * NC

    def hello(i, _):
        j = lax.rem(me + i, plane)
        to = dev(x, (j // NC) % NY, j // (NC * NY), j % NC)
        pl.semaphore_signal(bar, inc=1, device_id=to, device_id_type=MESH)
        return 0

    lax.fori_loop(1, plane, hello, 0)
    pl.semaphore_signal(bar, inc=1, device_id=right, device_id_type=MESH)
    pl.semaphore_signal(bar, inc=1, device_id=left, device_id_type=MESH)
    pl.semaphore_wait(bar, plane + 1)

    src_slot = (z_hi % 2) * 8 + y * NC + c
    src_rows = pl.ds(pl.multiple_of(src_slot * piece, 64), piece)

    def a_send(n, _):
        q = n // NY
        dz = (1 + 2 * (q // 2)) * (1 - 2 * (q % 2))
        tz, ty = lax.rem(z + dz + NZ, NZ), lax.rem(y + n % NY, NY)
        lanes = pl.ds(pl.multiple_of((ty * 4 + tz // 2) * 128, 128), 128)
        send(w_hbm.at[pl.ds(0, 2), :, lanes], gu.at[0, :, src_rows, :], a_ss, a_rs.at[src_slot],
             dev(x, ty, tz, z_hi // 2))
        return 0

    lax.fori_loop(0, 16, a_send, 0)

    wz, wc = 2 * z_hi + y // 2, y % 2
    w_dst = wd.at[0, pl.ds(pl.multiple_of(c * piece, 64), piece),
                  pl.ds(pl.multiple_of(z_lo * 512, 128), 512)]
    for j in range(NY):
        ty = lax.rem(y + j, NY)
        src = w_hbm.at[2, :, pl.ds(pl.multiple_of(ty * 512, 128), 512)]
        rs = w_rs.at[z_lo * NC + c]
        if j == 0:
            here = jnp.logical_and(wz == z, wc == c)

            @pl.when(here)
            def _():
                pltpu.make_async_copy(src, w_dst, rs).start()

            @pl.when(jnp.logical_not(here))
            def _():
                send(src, w_dst, w_ss.at[0], rs, dev(x, ty, wz, wc))
        else:
            send(src, w_dst, w_ss.at[j], rs, dev(x, ty, wz, wc))

    for k, to in ((0, up), (1, down)):
        r = pl.ds(k * hrows, hrows)
        send(tok_hbm.at[r, mycols], tok.at[z_lo, r], tk_ss.at[k], tk_rs.at[k], to)

    same = 1 - (z_hi // 2 + c) % 2
    m0 = (z_hi + 1 + same) % 2

    def slot_of(n):
        return ((m0 + n // 4) % 2) * 8 + lax.rem(y - n % 4 + NY, NY) * NC

    def pc(k, s):
        return gu.at[k, :, pl.ds(pl.multiple_of(s * piece, 64), piece), :]

    def x_own(n):
        for core in range(NC):
            s = slot_of(n) + core
            take(pc(0, s), a_rs.at[s])
            send(pc(0, s), pc(1, s), xo_ss.at[0], x_rs.at[0, s], right)
            send(pc(0, s), pc(2, s), xo_ss.at[1], x_rs.at[1, s], left)

    def x_fwd(n):
        s = slot_of(n)
        take(pc(1, s), x_rs.at[0, s])
        send(pc(1, s), pc(3, s), xf_ss.at[0], x_rs.at[2, s], right)
        take(pc(2, s + 1), x_rs.at[1, s + 1])
        send(pc(2, s + 1), pc(3, s + 1), xf_ss.at[1], x_rs.at[2, s + 1], left)

    lag = 2
    for n in range(lag):
        x_own(n)

    def x_loop(n, _):
        x_own(n)
        x_fwd(n - lag)
        return 0

    lax.fori_loop(lag, 8, x_loop, 0)

    def wpc(k, i):
        return wd.at[k, pl.ds((i % NC) * piece, piece), pl.ds((i // NC) * 512, 512)]

    for i in range(4):
        take(wpc(0, i), w_rs.at[i])
        send(wpc(0, i), wpc(1, i), wo_ss.at[0], wx_rs.at[0, i], right)
        send(wpc(0, i), wpc(2, i), wo_ss.at[1], wx_rs.at[1, i], left)
    for n in range(8 - lag, 8):
        x_fwd(n)

    load.wait()
    for k in range(2):
        r = pl.ds(k * hrows, hrows)
        take(tok.at[1 - z_lo, r], tk_rs.at[k])

    lane = pl.ds(pl.multiple_of(((1 - z_lo) * 4 + z_hi) * 128, 128), 128)

    def gate_up(r):
        if r == 1:
            for n in range(8):
                take(pc(1, 2 * n + 1), x_rs.at[0, 2 * n + 1])
        if r == 2:
            for n in range(8):
                take(pc(2, 2 * n), x_rs.at[1, 2 * n])
        if r == 3:
            for n in range(16):
                take(pc(3, n), x_rs.at[2, n])
        rhs = jnp.concatenate([gu[r, 0], gu[r, 1]], axis=1)
        px[r] = jnp.dot(tok[1 - c], rhs, preferred_element_type=jnp.float32)
        send(px.at[r], pr.at[r], p_ss.at[r], p_rs.at[r], sib)
        po[...] = jnp.dot(tok[c], rhs, preferred_element_type=jnp.float32)
        take(pr.at[r], p_rs.at[r])
        gate = po[:, :128] + pr[r, :, :128]
        upv = po[:, 128:] + pr[r, :, 128:]
        hid[c, r, :, lane] = (gate / (1.0 + jnp.exp(-gate)) * upv).astype(jnp.bfloat16)
        own = hid.at[c, r, :, lane]
        send(own, own, h_ss.at[r, 0, 0], h_rs.at[r, 0, 1], up)
        send(own, own, h_ss.at[r, 1, 0], h_rs.at[r, 1, 1], down)
        send(own, own, s_ss.at[r], s_rs.at[r], sib)

    def ring(r, d):
        for k, to in ((0, up), (1, down)):
            zs = lax.rem(z + (d if k else NZ - d), NZ)
            ln = pl.ds(pl.multiple_of(((1 - zs % 2) * 4 + zs // 2) * 128, 128), 128)
            part = pl.ds(k * hrows, hrows)
            got = hid.at[c, r, part, ln] if d == 4 else hid.at[c, r, :, ln]
            take(got, h_rs.at[r, k, d])
            if d < 3:
                send(got, got, h_ss.at[r, k, d], h_rs.at[r, k, d + 1], to)
            elif d == 3:
                more = hid.at[c, r, part, ln]
                send(more, more, h_ss.at[r, k, d], h_rs.at[r, k, d + 1], to)
            send(got, got, s_ss.at[r], s_rs.at[r], sib)

    def wd_fwd():
        for i in range(0, 4, 2):
            take(wpc(1, i), wx_rs.at[0, i])
            send(wpc(1, i), wpc(3, i), wf_ss.at[0], wx_rs.at[2, i], right)
            take(wpc(2, i + 1), wx_rs.at[1, i + 1])
            send(wpc(2, i + 1), wpc(3, i + 1), wf_ss.at[1], wx_rs.at[2, i + 1], left)

    def project(r):
        take(hid.at[1 - c, r], s_rs.at[r])
        if r == 1:
            for i in (1, 3):
                take(wpc(1, i), wx_rs.at[0, i])
        if r == 2:
            for i in (0, 2):
                take(wpc(2, i), wx_rs.at[1, i])
        if r == 3:
            for i in range(4):
                take(wpc(3, i), wx_rs.at[2, i])
        for g in range(2):
            term = lax.dot_general(hid[g, r], wd[r], (((1,), (1,)), ((), ())),
                                   preferred_element_type=jnp.float32)
            if r == 0:
                acc[g, pl.ds(0, rows)] = term
            else:
                acc[g, pl.ds(0, rows)] += term

    gate_up(0)
    gate_up(1)
    ring(0, 1)
    gate_up(2)
    ring(0, 2)
    ring(1, 1)
    gate_up(3)
    ring(0, 3)
    ring(1, 2)
    ring(2, 1)
    wd_fwd()
    ring(0, 4)
    ring(1, 3)
    ring(2, 2)
    ring(3, 1)
    project(0)
    ring(1, 4)
    ring(2, 3)
    ring(3, 2)
    project(1)
    ring(2, 4)
    ring(3, 3)
    project(2)
    ring(3, 4)
    project(3)

    acc[:, pl.ds(rows, 8)] = jnp.zeros((2, 8, dcols), jnp.float32)
    for ty in range(NY):
        for k in range(16):
            g, th, tc = k // 8, (k % 8) // 2, k % 2
            first = ((th * NY + ty) * NC + tc) * OWN
            st[ty, pl.ds(k * PAD, PAD)] = acc[g, pl.ds(first, PAD)].astype(jnp.bfloat16)
    for d in range(1, NY):
        ty = lax.rem(y + d, NY)
        send(st.at[ty], rv.at[3 - d], r_ss.at[d - 1], r_rs.at[3 - d], dev(x, ty, z, c))
    for k in range(3):
        take(rv.at[k], r_rs.at[k])
    total = st[y].astype(jnp.float32)
    for k in range(3):
        total += rv[k].astype(jnp.float32)
    fin[...] = total.astype(jnp.bfloat16)

    cols = pl.ds(pl.multiple_of((z * NC + c) * dcols, 128), dcols)

    def place(k, _):
        tz, tc = 2 * ((k % 8) // 2) + k // 8, k % 2
        src = fin.at[pl.ds(pl.multiple_of(k * PAD, PAD), PAD)]
        here = jnp.logical_and(tz == z, tc == c)

        @pl.when(here)
        def _():
            pltpu.make_async_copy(src, fo.at[:, cols], f_rs).start()

        @pl.when(jnp.logical_not(here))
        def _():
            send(src, fo.at[:, cols], f_ss, f_rs, dev(x, y, tz, tc))

        return 0

    lax.fori_loop(0, 16, place, 0)
    take(fo, f_rs)
    out_ref[...] = fo[...]

    take(w_hbm.at[pl.ds(0, 2)], a_ss)
    for j in range(NY):
        src = w_hbm.at[2, :, pl.ds(0, 512)]
        if j == 0:
            @pl.when(jnp.logical_not(jnp.logical_and(wz == z, wc == c)))
            def _():
                take(src, w_ss.at[0])
        else:
            take(src, w_ss.at[j])
    for k in range(2):
        take(tok.at[0, pl.ds(0, hrows)], tk_ss.at[k])
        take(gu.at[0], xo_ss.at[k])
        take(gu.at[0, 0], xf_ss.at[k])
        take(wd.at[0], wo_ss.at[k])
        take(wd.at[0, pl.ds(0, piece)], wf_ss.at[k])
    for r in range(4):
        take(px.at[r], p_ss.at[r])
        take(hid.at[c, r], s_ss.at[r])
        for k in range(2):
            for d in range(4):
                h = hrows if d == 3 else rows
                take(hid.at[c, r, pl.ds(0, h), lane], h_ss.at[r, k, d])
    for k in range(3):
        take(rv.at[k], r_ss.at[k])
    take(fin.at[pl.ds(0, 15 * PAD)], f_ss)


def per_device(tokens, routes, route_weights, ffn_weights):
    rows, width = tokens.shape
    w = ffn_weights.reshape(ffn_weights.shape[1], ffn_weights.shape[2], ffn_weights.shape[4])
    piece = w.shape[1]
    half = width // 2
    dcols = width // 16
    bf, f32 = jnp.bfloat16, jnp.float32
    dma = pltpu.SemaphoreType.DMA
    summed = pl.pallas_call(
        kernel,
        out_shape=jax.ShapeDtypeStruct((PAD, width), bf),
        in_specs=[pl.BlockSpec(memory_space=pl.ANY)] * 2,
        out_specs=pl.BlockSpec(memory_space=pltpu.VMEM),
        scratch_shapes=[
            pltpu.VMEM((2, rows, half), bf),
            pltpu.VMEM((4, 2, half, 128), bf),
            pltpu.VMEM((4, 2 * piece, 1024), bf),
            pltpu.VMEM((4, rows, 256), f32),
            pltpu.VMEM((4, rows, 256), f32),
            pltpu.VMEM((rows, 256), f32),
            pltpu.VMEM((2, 4, rows, 1024), bf),
            pltpu.VMEM((2, rows + 8, dcols), f32),
            pltpu.VMEM((NY, 16 * PAD, dcols), bf),
            pltpu.VMEM((3, 16 * PAD, dcols), bf),
            pltpu.VMEM((16 * PAD, dcols), bf),
            pltpu.VMEM((PAD, width), bf),
            dma,
            dma((2,)),
            dma((2,)),
            dma,
            dma((16,)),
            dma((2,)),
            dma((3, 16)),
            dma((2,)),
            dma((4,)),
            dma((4,)),
            dma((2,)),
            dma((3, 4)),
            dma((2,)),
            dma((4,)),
            dma((4,)),
            dma((4, 2, 4)),
            dma((4, 2, 5)),
            dma((4,)),
            dma((4,)),
            dma((3,)),
            dma((3,)),
            dma,
            dma,
        ],
        compiler_params=pltpu.CompilerParams(
            collective_id=0, has_side_effects=True, vmem_limit_bytes=56 * 2**20
        ),
    )(tokens, w)
    first = lax.axis_index("tp") * OWN
    matched = lax.dynamic_slice_in_dim(routes, first, OWN) == 0
    weights = lax.dynamic_slice_in_dim(route_weights, first, OWN)
    mix = jnp.sum(jnp.where(matched, weights, 0.0), axis=1)
    return (summed[:OWN].astype(f32) * mix[:, None]).astype(bf)


def solution(mesh):
    placed = (
        P("group", None),
        P("group", None),
        P("group", None),
        P(None, None, "tp", "group", None),
    )
    return jax.shard_map(
        per_device, mesh=mesh, in_specs=placed, out_specs=P(("group", "tp"), None), check_vma=False
    )
```

time: 494 us -> 168 us (0.34)
  the two profiles are of different devices: /device:TPU:169 before, /device:TPU:33 now
where the time goes in v1:
time: 168 us; the launch traced here: 167 us
  Pallas kernels  164 us (98%)
  other arithmetic  2.49 us (1%)
    pallas_call x1, Pallas kernels, per_device(): pl.pallas_call(kernel, out_shape=jax.ShapeDtypeStruct((PAD, width), bf),...  164 us

profile of v1, /device:TPU:33, one launch (start us, length us, event | category | flops | bytes accessed | tf_op | source)
XLA Modules:
  0.0 166.9 jit_solution(509169303027724354)
XLA Ops:
  0.0 0.8 fusion
  0.8 164.4 %shard_map.46 = bf16[16,6144]{1,0:T(8,128)(2,1)} custom-call(bf16[448,6144]{1,0:T(8,128)(2,1)} %tok_hbm.1, bf16[3,192,2048]{2,1,0:T(8,128)(2,1)} %bitcast.1), custom_call_target="tpu_custom_call" | custom-call | tf_op jit(solution)/shard_map/pallas_call | solution.py:313
  165.2 1.7 %multiply_convert_fusion = bf16[14,6144]{1,0:T(8,128)(2,1)} fusion(f32[14]{0:T(128)S(1)} %fusion, bf16[16,6144]{1,0:T(8,128)(2,1)} %shard_map.46), kind=kLoop, calls=%fused_computation | loop fusion | flops 258048 | bytes 344120 | tf_op jit(solution)/shard_map/convert_element_type | solution.py:363

commit v2 on v1

v2 whole, which is shorter than its diff:
```python
import jax
import jax.numpy as jnp
from jax import lax
from jax.experimental import pallas as pl
from jax.experimental.pallas import tpu as pltpu
from jax.sharding import PartitionSpec as P

MESH = pl.DeviceIdType.MESH
NX, NY, NZ, NC = 4, 4, 8, 2
OWN = 14
PAD = 16


def dev(x, y, z, c):
    x, y, z = lax.rem(x + 2 * NX, NX), lax.rem(y + 2 * NY, NY), lax.rem(z + 2 * NZ, NZ)
    return ((z % 2) * NX + x, ((z // 2) * NY + y) * NC + c)


def take(ref, sem):
    pltpu.make_async_copy(ref, ref, sem).wait()


def kernel(tok_hbm, w_hbm, out_ref, tok, gu, wd, px, pr, po, hid, acc, st, rv, fin, fo,
           tok_sem, tk_ss, tk_rs, a_ss, a_rs, xo_ss, x_rs, xf_ss, w_ss, w_rs, wo_ss, wx_rs, wf_ss,
           p_ss, p_rs, h_ss, h_rs, s_ss, s_rs, r_ss, r_rs, f_ss, f_rs, ty_ss, ty_rs):
    grp, tp = lax.axis_index("group"), lax.axis_index("tp")
    z_lo, x = grp // NX, grp % NX
    c, y, z_hi = tp % NC, (tp // NC) % NY, tp // (NC * NY)
    z = z_hi * 2 + z_lo
    rows = tok.shape[1]
    half = tok.shape[2]
    piece = w_hbm.shape[1]
    hrows = rows // 2
    dcols = acc.shape[2]

    def send(src, dst, ss, rs, to):
        pltpu.make_async_remote_copy(
            src_ref=src, dst_ref=dst, send_sem=ss, recv_sem=rs, device_id=to, device_id_type=MESH
        ).start()

    right, left = dev(x + 1, y, z, c), dev(x - 1, y, z, c)
    up, down = dev(x, y, z + 1, c), dev(x, y, z - 1, c)
    sib = dev(x, y, z, 1 - c)
    chunk = half // 4

    def at_hbm(k):
        return pl.ds(pl.multiple_of((2 * k + c) * chunk, 128), chunk)

    for k in range(4):
        pltpu.make_async_copy(
            tok_hbm.at[:, at_hbm(k)], tok.at[z_lo, :, pl.ds(k * chunk, chunk)], tok_sem
        ).start()

    bar = pltpu.get_barrier_semaphore()
    me = (z * NY + y) * NC + c
    plane = NZ * NY * NC

    def hello(i, _):
        j = lax.rem(me + i, plane)
        to = dev(x, (j // NC) % NY, j // (NC * NY), j % NC)
        pl.semaphore_signal(bar, inc=1, device_id=to, device_id_type=MESH)
        return 0

    lax.fori_loop(1, plane, hello, 0)
    pl.semaphore_signal(bar, inc=1, device_id=right, device_id_type=MESH)
    pl.semaphore_signal(bar, inc=1, device_id=left, device_id_type=MESH)
    pl.semaphore_wait(bar, plane + 1)

    src_slot = z_hi * 4 + (y % 2) * NC + c
    src_rows = pl.ds(pl.multiple_of(src_slot * piece, 64), piece)

    def a_wave(w):
        far = 1 + 2 * (w // 2)
        for dy in (w % 2, w % 2 + 2):
            for dz in (far, -far):
                ty, tz = lax.rem(y + dy, NY), lax.rem(z + dz + NZ, NZ)
                lanes = pl.ds(pl.multiple_of((ty * 4 + tz // 2) * 128, 128), 128)
                send(w_hbm.at[pl.ds(0, 2), :, lanes], gu.at[0, :, src_rows, :], a_ss,
                     a_rs.at[src_slot], dev(x, ty, tz, y // 2))

    wz, wc = 2 * z_hi + c, y // 2
    w_here = jnp.logical_and(wz == z, wc == c)
    w_dst = wd.at[0, pl.ds(pl.multiple_of((y % 2) * piece, 64), piece),
                  pl.ds(pl.multiple_of(z_lo * 512, 128), 512)]

    def w_send():
        for j in range(NY):
            ty = lax.rem(y + j, NY)
            src = w_hbm.at[2, :, pl.ds(pl.multiple_of(ty * 512, 128), 512)]
            rs = w_rs.at[z_lo * 2 + y % 2]
            if j == 0:
                @pl.when(w_here)
                def _():
                    pltpu.make_async_copy(src, w_dst, rs).start()

                @pl.when(jnp.logical_not(w_here))
                def _():
                    send(src, w_dst, w_ss.at[0], rs, dev(x, ty, wz, wc))
            else:
                send(src, w_dst, w_ss.at[j], rs, dev(x, ty, wz, wc))

    quarter = rows // NY

    def quarter_of(yy):
        return pl.ds(pl.multiple_of(yy * quarter, PAD), quarter)

    def tok_send():
        for k in range(4):
            send(tok_hbm.at[quarter_of(y), at_hbm(k)],
                 tok.at[z_lo, quarter_of(y), pl.ds(k * chunk, chunk)],
                 tk_ss.at[k // 2], tk_rs.at[k // 2], down if k // 2 else up)

    def tok_pass():
        for k in range(2):
            take(tok.at[1 - z_lo, quarter_of(y), pl.ds(2 * k * chunk, 2 * chunk)], tk_rs.at[k])
        for d in range(1, NY):
            mine = tok.at[1 - z_lo, quarter_of(y)]
            send(mine, mine, ty_ss.at[d - 1], ty_rs.at[d - 1], dev(x, y + d, z, c))

    def tok_wait():
        take(tok.at[z_lo], tok_sem)
        for d in range(1, NY):
            take(tok.at[1 - z_lo, quarter_of(lax.rem(y - d + NY, NY))], ty_rs.at[d - 1])

    def slot_of(w, m):
        far = (1 + 2 * (w // 2)) * (1 - 2 * m)
        return (lax.rem(z - far + NZ, NZ) // 2) * 4 + ((y + w) % 2) * NC

    def pc(k, s):
        return gu.at[k, :, pl.ds(pl.multiple_of(s * piece, 64), piece), :]

    def x_own(w):
        for m in range(2):
            for core in range(NC):
                s = slot_of(w, m) + core
                take(pc(0, s), a_rs.at[s])
                send(pc(0, s), pc(1, s), xo_ss.at[0], x_rs.at[0, s], right)
                send(pc(0, s), pc(2, s), xo_ss.at[1], x_rs.at[1, s], left)

    def x_fwd(w):
        for m in range(2):
            s = slot_of(w, m)
            take(pc(1, s), x_rs.at[0, s])
            send(pc(1, s), pc(3, s), xf_ss.at[0], x_rs.at[2, s], right)
            take(pc(2, s + 1), x_rs.at[1, s + 1])
            send(pc(2, s + 1), pc(3, s + 1), xf_ss.at[1], x_rs.at[2, s + 1], left)

    def wpc(k, i):
        return wd.at[k, pl.ds(pl.multiple_of((i % 2) * piece, 64), piece),
                     pl.ds(pl.multiple_of((i // 2) * 512, 128), 512)]

    near = z_lo * 2
    far = 2 - near

    def w_own(first):
        for i in (first, first + 1):
            take(wpc(0, i), w_rs.at[i])
            send(wpc(0, i), wpc(1, i), wo_ss.at[0], wx_rs.at[0, i], right)
            send(wpc(0, i), wpc(2, i), wo_ss.at[1], wx_rs.at[1, i], left)

    def w_fwd(i):
        take(wpc(1, i), wx_rs.at[0, i])
        send(wpc(1, i), wpc(3, i), wf_ss.at[0], wx_rs.at[2, i], right)
        take(wpc(2, i + 1), wx_rs.at[1, i + 1])
        send(wpc(2, i + 1), wpc(3, i + 1), wf_ss.at[1], wx_rs.at[2, i + 1], left)

    lane = pl.ds(pl.multiple_of(((1 - z_lo) * 4 + z_hi) * 128, 128), 128)

    def gate_up(r):
        if r == 1:
            for n in range(8):
                take(pc(1, 2 * n + 1), x_rs.at[0, 2 * n + 1])
        if r == 2:
            for n in range(8):
                take(pc(2, 2 * n), x_rs.at[1, 2 * n])
        if r == 3:
            for n in range(16):
                take(pc(3, n), x_rs.at[2, n])
        rhs = jnp.concatenate([gu[r, 0], gu[r, 1]], axis=1)
        px[r] = jnp.dot(tok[1 - c], rhs, preferred_element_type=jnp.float32)
        send(px.at[r], pr.at[r], p_ss.at[r], p_rs.at[r], sib)
        po[...] = jnp.dot(tok[c], rhs, preferred_element_type=jnp.float32)
        take(pr.at[r], p_rs.at[r])
        gate = po[:, :128] + pr[r, :, :128]
        upv = po[:, 128:] + pr[r, :, 128:]
        hid[c, r, :, lane] = (gate / (1.0 + jnp.exp(-gate)) * upv).astype(jnp.bfloat16)
        own = hid.at[c, r, :, lane]
        send(own, own, h_ss.at[r, 0, 0], h_rs.at[r, 0, 1], up)
        send(own, own, h_ss.at[r, 1, 0], h_rs.at[r, 1, 1], down)
        send(own, own, s_ss.at[r], s_rs.at[r], sib)

    def ring(r, d):
        for k, to in ((0, up), (1, down)):
            zs = lax.rem(z + (d if k else NZ - d), NZ)
            ln = pl.ds(pl.multiple_of(((1 - zs % 2) * 4 + zs // 2) * 128, 128), 128)
            part = pl.ds(k * hrows, hrows)
            got = hid.at[c, r, part, ln] if d == 4 else hid.at[c, r, :, ln]
            take(got, h_rs.at[r, k, d])
            if d < 3:
                send(got, got, h_ss.at[r, k, d], h_rs.at[r, k, d + 1], to)
            elif d == 3:
                more = hid.at[c, r, part, ln]
                send(more, more, h_ss.at[r, k, d], h_rs.at[r, k, d + 1], to)
            send(got, got, s_ss.at[r], s_rs.at[r], sib)

    def ready(r):
        take(hid.at[1 - c, r], s_rs.at[r])
        if r == 1:
            for i in (1, 3):
                take(wpc(1, i), wx_rs.at[0, i])
        if r == 2:
            for i in (0, 2):
                take(wpc(2, i), wx_rs.at[1, i])
        if r == 3:
            for i in range(4):
                take(wpc(3, i), wx_rs.at[2, i])

    def project(r, g):
        term = lax.dot_general(hid[g, r], wd[r], (((1,), (1,)), ((), ())),
                               preferred_element_type=jnp.float32)
        if r == 0:
            acc[g, pl.ds(0, rows)] = term
        else:
            acc[g, pl.ds(0, rows)] += term

    acc[:, pl.ds(rows, 8)] = jnp.zeros((2, 8, dcols), jnp.float32)
    a_wave(0)
    pl.when(c == z_lo)(w_send)
    x_own(0)
    tok_send()
    w_own(near)
    tok_pass()
    a_wave(1)
    a_wave(2)
    pl.when(c != z_lo)(w_send)
    x_own(1)
    a_wave(3)
    x_fwd(0)
    x_fwd(1)
    w_fwd(near)
    x_own(2)
    x_fwd(2)
    x_own(3)
    tok_wait()
    gate_up(0)
    ring(0, 1)
    x_fwd(3)
    w_own(far)
    ring(0, 2)
    gate_up(1)
    gate_up(2)
    ring(0, 3)
    gate_up(3)
    ring(1, 1)
    ring(2, 1)
    ring(3, 1)
    ring(0, 4)
    ring(1, 2)
    ring(2, 2)
    ring(3, 2)
    w_fwd(far)
    ring(1, 3)
    ring(2, 3)
    ring(3, 3)
    ready(0)
    project(0, 0)
    project(0, 1)
    ring(1, 4)
    ring(2, 4)
    ready(1)
    project(1, 0)
    project(1, 1)
    ring(3, 4)
    ready(2)
    project(2, 0)
    project(2, 1)
    ready(3)

    for g in range(2):
        project(3, g)
        for ty in range(NY):
            for k in range(8):
                first = (((k // 2) * NY + ty) * NC + k % 2) * OWN
                st[g, ty, pl.ds(k * PAD, PAD)] = acc[g, pl.ds(first, PAD)].astype(jnp.bfloat16)
        for d in range(1, NY):
            ty = lax.rem(y + d, NY)
            send(st.at[g, ty], rv.at[g, 3 - d], r_ss.at[g, d - 1], r_rs.at[g, 3 - d], dev(x, ty, z, c))

    cols = pl.ds(pl.multiple_of((z * NC + c) * dcols, 128), dcols)
    for g in range(2):
        total = st[g, y].astype(jnp.float32)
        for k in range(3):
            take(rv.at[g, k], r_rs.at[g, k])
            total += rv[g, k].astype(jnp.float32)
        fin[g] = total.astype(jnp.bfloat16)

        def place(k, _):
            tz, tc = 2 * (k // 2) + g, k % 2
            src = fin.at[g, pl.ds(pl.multiple_of(k * PAD, PAD), PAD)]
            here = jnp.logical_and(tz == z, tc == c)

            @pl.when(here)
            def _():
                pltpu.make_async_copy(src, fo.at[:, cols], f_rs).start()

            @pl.when(jnp.logical_not(here))
            def _():
                send(src, fo.at[:, cols], f_ss, f_rs, dev(x, y, tz, tc))

            return 0

        lax.fori_loop(0, 8, place, 0)
    take(fo, f_rs)
    for n in range(2 * NZ * NC):
        zh, yy, core = n // 8, (n // 2) % 4, n % 2
        at = (((2 * zh + core) * NC + yy // 2) * 2 + yy % 2) * piece
        out_ref[:, n * piece:(n + 1) * piece] = fo[:, at:at + piece]

    take(w_hbm.at[pl.ds(0, 2)], a_ss)
    for j in range(NY):
        src = w_hbm.at[2, :, pl.ds(0, 512)]
        if j == 0:
            @pl.when(jnp.logical_not(w_here))
            def _():
                take(src, w_ss.at[0])
        else:
            take(src, w_ss.at[j])
    for k in range(2):
        take(tok.at[0, pl.ds(0, quarter), pl.ds(0, 2 * chunk)], tk_ss.at[k])
        take(gu.at[0], xo_ss.at[k])
        take(gu.at[0, 0], xf_ss.at[k])
        take(wd.at[0], wo_ss.at[k])
        take(wd.at[0, pl.ds(0, piece)], wf_ss.at[k])
    for r in range(4):
        take(px.at[r], p_ss.at[r])
        take(hid.at[c, r], s_ss.at[r])
        for k in range(2):
            for d in range(4):
                h = hrows if d == 3 else rows
                take(hid.at[c, r, pl.ds(0, h), lane], h_ss.at[r, k, d])
    for k in range(3):
        take(tok.at[0, pl.ds(0, quarter)], ty_ss.at[k])
        for g in range(2):
            take(rv.at[g, k], r_ss.at[g, k])
    take(fin.at[0], f_ss)
    take(fin.at[1, pl.ds(0, 7 * PAD)], f_ss)


def per_device(tokens, routes, route_weights, ffn_weights):
    rows, width = tokens.shape
    w = ffn_weights.reshape(ffn_weights.shape[1], ffn_weights.shape[2], ffn_weights.shape[4])
    piece = w.shape[1]
    half = width // 2
    dcols = width // 16
    bf, f32 = jnp.bfloat16, jnp.float32
    dma = pltpu.SemaphoreType.DMA
    summed = pl.pallas_call(
        kernel,
        out_shape=jax.ShapeDtypeStruct((PAD, width), bf),
        in_specs=[pl.BlockSpec(memory_space=pl.ANY)] * 2,
        out_specs=pl.BlockSpec(memory_space=pltpu.VMEM),
        scratch_shapes=[
            pltpu.VMEM((2, rows, half), bf),
            pltpu.VMEM((4, 2, half, 128), bf),
            pltpu.VMEM((4, 2 * piece, 1024), bf),
            pltpu.VMEM((4, rows, 256), f32),
            pltpu.VMEM((4, rows, 256), f32),
            pltpu.VMEM((rows, 256), f32),
            pltpu.VMEM((2, 4, rows, 1024), bf),
            pltpu.VMEM((2, rows + 8, dcols), f32),
            pltpu.VMEM((2, NY, 8 * PAD, dcols), bf),
            pltpu.VMEM((2, 3, 8 * PAD, dcols), bf),
            pltpu.VMEM((2, 8 * PAD, dcols), bf),
            pltpu.VMEM((PAD, width), bf),
            dma,
            dma((2,)),
            dma((2,)),
            dma,
            dma((16,)),
            dma((2,)),
            dma((3, 16)),
            dma((2,)),
            dma((4,)),
            dma((4,)),
            dma((2,)),
            dma((3, 4)),
            dma((2,)),
            dma((4,)),
            dma((4,)),
            dma((4, 2, 4)),
            dma((4, 2, 5)),
            dma((4,)),
            dma((4,)),
            dma((2, 3)),
            dma((2, 3)),
            dma,
            dma,
            dma((3,)),
            dma((3,)),
        ],
        compiler_params=pltpu.CompilerParams(
            collective_id=0, has_side_effects=True, vmem_limit_bytes=56 * 2**20
        ),
    )(tokens, w)
    first = lax.axis_index("tp") * OWN
    matched = lax.dynamic_slice_in_dim(routes, first, OWN) == 0
    weights = lax.dynamic_slice_in_dim(route_weights, first, OWN)
    mix = jnp.sum(jnp.where(matched, weights, 0.0), axis=1)
    return (summed[:OWN].astype(f32) * mix[:, None]).astype(bf)


def solution(mesh):
    placed = (
        P("group", None),
        P("group", None),
        P("group", None),
        P(None, None, "tp", "group", None),
    )
    return jax.shard_map(
        per_device, mesh=mesh, in_specs=placed, out_specs=P(("group", "tp"), None), check_vma=False
    )
```

time: 168 us -> 144 us (0.86)
  Pallas kernels: 164 us -> 142 us
    pallas_call x1, Pallas kernels: 164 us -> 142 us  [per_device(): pl.pallas_call(kernel, out_shape=jax.ShapeDtypeStruct((PAD, width), bf),...]
where the time goes in v2:
time: 144 us
  Pallas kernels  142 us (99%)
  other arithmetic  2.49 us (2%)
    pallas_call x1, Pallas kernels, per_device(): pl.pallas_call(kernel, out_shape=jax.ShapeDtypeStruct((PAD, width), bf),...  142 us

profile of v2, /device:TPU:33, one launch (start us, length us, event | category | flops | bytes accessed | tf_op | source)
XLA Modules:
  0.0 144.1 jit_solution(424979731346273454)
XLA Ops:
  0.0 0.8 fusion
  0.8 141.6 %shard_map.46 = bf16[16,6144]{1,0:T(8,128)(2,1)} custom-call(bf16[448,6144]{1,0:T(8,128)(2,1)} %tok_hbm.1, bf16[3,192,2048]{2,1,0:T(8,128)(2,1)} %bitcast.1), custom_call_target="tpu_custom_call" | custom-call | tf_op jit(solution)/shard_map/pallas_call | solution.py:357
  142.4 1.7 %multiply_convert_fusion = bf16[14,6144]{1,0:T(8,128)(2,1)} fusion(f32[14]{0:T(128)S(1)} %fusion, bf16[16,6144]{1,0:T(8,128)(2,1)} %shard_map.46), kind=kLoop, calls=%fused_computation | loop fusion | flops 258048 | bytes 344120 | tf_op jit(solution)/shard_map/convert_element_type | solution.py:409

commit v3 on v2

--- a/solution.py
+++ b/solution.py
@@ -40,6 +40,7 @@
 
     right, left = dev(x + 1, y, z, c), dev(x - 1, y, z, c)
     up, down = dev(x, y, z + 1, c), dev(x, y, z - 1, c)
+    north, south = dev(x, y + 1, z, c), dev(x, y - 1, z, c)
     sib = dev(x, y, z, 1 - c)
     chunk = half // 4
 
@@ -113,14 +114,22 @@
     def tok_pass():
         for k in range(2):
             take(tok.at[1 - z_lo, quarter_of(y), pl.ds(2 * k * chunk, 2 * chunk)], tk_rs.at[k])
-        for d in range(1, NY):
-            mine = tok.at[1 - z_lo, quarter_of(y)]
-            send(mine, mine, ty_ss.at[d - 1], ty_rs.at[d - 1], dev(x, y + d, z, c))
+        mine = tok.at[1 - z_lo, quarter_of(y)]
+        send(mine, mine, ty_ss.at[0], ty_rs.at[0], north)
+        send(mine, mine, ty_ss.at[1], ty_rs.at[1], south)
+
+    def tok_fwd():
+        for k, to in ((0, north), (1, south)):
+            yy = quarter_of(lax.rem(y + (1 if k else NY - 1), NY))
+            take(tok.at[1 - z_lo, yy], ty_rs.at[k])
+            part = tok.at[1 - z_lo, yy, pl.ds(2 * k * chunk, 2 * chunk)]
+            send(part, part, ty_ss.at[2 + k], ty_rs.at[2 + k], to)
 
     def tok_wait():
         take(tok.at[z_lo], tok_sem)
-        for d in range(1, NY):
-            take(tok.at[1 - z_lo, quarter_of(lax.rem(y - d + NY, NY))], ty_rs.at[d - 1])
+        for k in range(2):
+            yy = quarter_of(lax.rem(y + 2, NY))
+            take(tok.at[1 - z_lo, yy, pl.ds(2 * k * chunk, 2 * chunk)], ty_rs.at[2 + k])
 
     def slot_of(w, m):
         far = (1 + 2 * (w // 2)) * (1 - 2 * m)
@@ -228,29 +237,29 @@
     pl.when(c == z_lo)(w_send)
     x_own(0)
     tok_send()
-    w_own(near)
+    a_wave(1)
     tok_pass()
-    a_wave(1)
     a_wave(2)
+    x_fwd(0)
+    x_own(1)
+    x_fwd(1)
+    a_wave(3)
+    tok_fwd()
+    x_own(2)
     pl.when(c != z_lo)(w_send)
-    x_own(1)
-    a_wave(3)
-    x_fwd(0)
-    x_fwd(1)
-    w_fwd(near)
-    x_own(2)
     x_fwd(2)
     x_own(3)
     tok_wait()
     gate_up(0)
+    x_fwd(3)
+    w_own(near)
     ring(0, 1)
-    x_fwd(3)
-    w_own(far)
     ring(0, 2)
     gate_up(1)
     gate_up(2)
     ring(0, 3)
     gate_up(3)
+    w_own(far)
     ring(1, 1)
     ring(2, 1)
     ring(3, 1)
@@ -258,10 +267,11 @@
     ring(1, 2)
     ring(2, 2)
     ring(3, 2)
-    w_fwd(far)
+    w_fwd(near)
     ring(1, 3)
     ring(2, 3)
     ring(3, 3)
+    w_fwd(far)
     ready(0)
     project(0, 0)
     project(0, 1)
@@ -338,8 +348,10 @@
             for d in range(4):
                 h = hrows if d == 3 else rows
                 take(hid.at[c, r, pl.ds(0, h), lane], h_ss.at[r, k, d])
+    for k in range(2):
+        take(tok.at[0, pl.ds(0, quarter)], ty_ss.at[k])
+        take(tok.at[0, pl.ds(0, quarter), pl.ds(0, 2 * chunk)], ty_ss.at[2 + k])
     for k in range(3):
-        take(tok.at[0, pl.ds(0, quarter)], ty_ss.at[k])
         for g in range(2):
             take(rv.at[g, k], r_ss.at[g, k])
     take(fin.at[0], f_ss)
@@ -395,8 +407,8 @@
             dma((2, 3)),
             dma,
             dma,
-            dma((3,)),
-            dma((3,)),
+            dma((4,)),
+            dma((4,)),
         ],
         compiler_params=pltpu.CompilerParams(
             collective_id=0, has_side_effects=True, vmem_limit_bytes=56 * 2**20

time: 144 us -> 138 us (0.958)
  Pallas kernels: 142 us -> 135 us
    pallas_call x1, Pallas kernels: 142 us -> 135 us  [per_device(): pl.pallas_call(kernel, out_shape=jax.ShapeDtypeStruct((PAD, width), bf),...]
where the time goes in v3:
time: 138 us
  Pallas kernels  135 us (98%)
  other arithmetic  2.49 us (2%)
    pallas_call x1, Pallas kernels, per_device(): pl.pallas_call(kernel, out_shape=jax.ShapeDtypeStruct((PAD, width), bf),...  135 us

profile of v3, /device:TPU:33, one launch (start us, length us, event | category | flops | bytes accessed | tf_op | source)
XLA Modules:
  0.0 137.6 jit_solution(8205102540681001409)
XLA Ops:
  0.0 0.8 fusion
  0.8 135.1 %shard_map.46 = bf16[16,6144]{1,0:T(8,128)(2,1)} custom-call(bf16[448,6144]{1,0:T(8,128)(2,1)} %tok_hbm.1, bf16[3,192,2048]{2,1,0:T(8,128)(2,1)} %bitcast.1), custom_call_target="tpu_custom_call" | custom-call | tf_op jit(solution)/shard_map/pallas_call | solution.py:369
  135.9 1.7 %multiply_convert_fusion = bf16[14,6144]{1,0:T(8,128)(2,1)} fusion(f32[14]{0:T(128)S(1)} %fusion, bf16[16,6144]{1,0:T(8,128)(2,1)} %shard_map.46), kind=kLoop, calls=%fused_computation | loop fusion | flops 258048 | bytes 344120 | tf_op jit(solution)/shard_map/convert_element_type | solution.py:421

commit v4 on v3

--- a/solution.py
+++ b/solution.py
@@ -254,13 +254,13 @@
     x_fwd(3)
     w_own(near)
     ring(0, 1)
+    gate_up(1)
     ring(0, 2)
-    gate_up(1)
     gate_up(2)
     ring(0, 3)
+    ring(1, 1)
     gate_up(3)
     w_own(far)
-    ring(1, 1)
     ring(2, 1)
     ring(3, 1)
     ring(0, 4)

time: 138 us -> 136 us (0.986)
    pallas_call x1, Pallas kernels: 135 us -> 134 us  [per_device(): pl.pallas_call(kernel, out_shape=jax.ShapeDtypeStruct((PAD, width), bf),...]
where the time goes in v4:
time: 136 us
  Pallas kernels  134 us (99%)
  other arithmetic  2.49 us (2%)
    pallas_call x1, Pallas kernels, per_device(): pl.pallas_call(kernel, out_shape=jax.ShapeDtypeStruct((PAD, width), bf),...  134 us

profile of v4, /device:TPU:33, one launch (start us, length us, event | category | flops | bytes accessed | tf_op | source)
XLA Modules:
  0.0 136.2 jit_solution(819883836406747714)
XLA Ops:
  0.0 0.8 fusion
  0.8 133.7 %shard_map.46 = bf16[16,6144]{1,0:T(8,128)(2,1)} custom-call(bf16[448,6144]{1,0:T(8,128)(2,1)} %tok_hbm.1, bf16[3,192,2048]{2,1,0:T(8,128)(2,1)} %bitcast.1), custom_call_target="tpu_custom_call" | custom-call | tf_op jit(solution)/shard_map/pallas_call | solution.py:369
  134.5 1.7 %multiply_convert_fusion = bf16[14,6144]{1,0:T(8,128)(2,1)} fusion(f32[14]{0:T(128)S(1)} %fusion, bf16[16,6144]{1,0:T(8,128)(2,1)} %shard_map.46), kind=kLoop, calls=%fused_computation | loop fusion | flops 258048 | bytes 344120 | tf_op jit(solution)/shard_map/convert_element_type | solution.py:421
